TPU v7x, 512 devices: a whole 4x4x16 slice. The times are simulated.
512 devices in a mesh: snap: 64 (over z, x), col: 8 (over y, core).
Axes of the slice: x: 4, y: 4, z: 16, core: 2. Of those that a mesh axis runs over, the one named last changes fastest.
Arguments:
- anomalies: bfloat16 [32768, 32768], P('snap', 'col'), may hold values from -16 to 16
- sketch_code: int32 [32768], P('col'), may hold values from 0 to 255
Outputs:
- scores: float32 [32768, 128], P('snap')
- eofs: float32 [32768, 128], P(('col', 'snap'))
All inputs are finite; a program needn't handle non-finite values.
Results may differ from a plain program's by a relative error of at most 0.0026.
Values may be sent and summed in bfloat16 or wider, within the bound.
A program may use at most 64 MiB of HBM per device.

v0:
```python
import jax
import jax.numpy as jnp
from jax import lax
from jax.sharding import PartitionSpec as P

RANK = 128


def sign_table(code, width):
    bucket = code % width
    sign = 1 - 2 * (code // width)
    hits = bucket[:, None] == lax.broadcasted_iota(jnp.int32, (code.shape[0], width), 1)
    return jnp.where(hits, sign[:, None], 0).astype(jnp.bfloat16)


def orthonormal(range_basis, gram):
    lower = jnp.linalg.cholesky(gram)
    return lax.linalg.triangular_solve(
        lower, range_basis, left_side=False, lower=True, transpose_a=True
    )


def per_device(anomalies, sketch_code):
    omega = sign_table(sketch_code, RANK)
    partial_sketch = jnp.dot(anomalies, omega, preferred_element_type=jnp.float32)
    sketch = lax.psum(partial_sketch, "col").astype(jnp.bfloat16)
    share_rows = anomalies.shape[1] // lax.axis_size("snap")
    local_basis = lax.dot_general(
        anomalies, sketch, (((0,), (0,)), ((), ())), preferred_element_type=jnp.float32
    )
    total_basis = lax.psum(local_basis, "snap")
    local_gram = jnp.dot(total_basis.T, total_basis, precision=lax.Precision.HIGHEST)
    gram = lax.psum(local_gram, "col")
    full_eofs = orthonormal(total_basis, gram)
    eofs = lax.dynamic_slice_in_dim(full_eofs, lax.axis_index("snap") * share_rows, share_rows, 0)
    basis = full_eofs.astype(jnp.bfloat16)
    partial_scores = jnp.dot(anomalies, basis, preferred_element_type=jnp.float32)
    scores = lax.psum(partial_scores, "col")
    return (scores, eofs)


def solution(mesh):
    return jax.shard_map(
        per_device,
        mesh=mesh,
        in_specs=(P("snap", "col"), P("col")),
        out_specs=(P("snap", None), P(("col", "snap"), None)),
        check_vma=False,
    )
```

profile of v0, /device:TPU:1, one launch (start us, length us, event | category | flops | bytes accessed | tf_op | source)
XLA Modules:
  0.0 514.3 jit_solution(8305312102552578149)
XLA Ops:
  7.2 0.0 all-reduce.5.cloned.1.call-start
  7.2 0.7 add_select_fusion.1
  8.0 5.1 convolution_bitcast_fusion.2
  13.1 29.8 %all-reduce.10 = bf16[512,128]{0,1:T(8,128)(2,1)S(1)} all-reduce(f32[512,128]{0,1:T(8,128)S(1)} %convolution_bitcast_fusion.2), channel_id=1, replica_groups=mesh['snap'=64,'col'=8] {'col'}, use_global_device_ids=true, to_apply=%region_0.1 | all-reduce | flops 65536 | bytes 393216 | tf_op jit(solution)/shard_map/psum | solution.py:26
  42.9 4.2 convolution_bitcast_fusion
  47.1 0.0 all-reduce.5.cloned.1.call-update
  47.1 0.0 all-reduce.7.cloned.1.call-start
  47.2 270.6 %all-reduce.5.cloned.1.call-done = f32[4096,128]{0,1:T(8,128)} async-done(((f32[4096,128]{0,1:T(8,128)}), f32[4096,128]{0,1:T(8,128)}) %all-reduce.5.cloned.1.call-update) | async-done | bytes 2097168 | tf_op jit(solution)/shard_map/psum | solution.py:31
  317.8 0.0 copy-start
  317.8 4.8 fusion.14
  322.6 0.0 all-reduce.7.cloned.1.call-update
  322.6 0.2 all-reduce.9.cloned.1.call-start
  322.8 77.1 %all-reduce.7.cloned.1.call-done = f32[128,128]{0,1:T(8,128)} async-done(((f32[128,128]{0,1:T(8,128)}), f32[128,128]{0,1:T(8,128)}) %all-reduce.7.cloned.1.call-update) | async-done | bytes 65552 | tf_op jit(solution)/shard_map/psum | solution.py:33
  399.9 0.9 copy.5
  400.8 0.9 fusion.8
  401.7 11.7 %cholesky.16 = f32[128,128]{1,0:T(8,128)S(1)} custom-call(f32[128,128]{1,0:T(8,128)S(1)} %fusion.8), custom_call_target="Cholesky" | custom-call | tf_op jit(solution)/shard_map/jit(cholesky)/cholesky | solution.py:17
  413.4 0.6 compare_reduce_fusion
  414.1 0.7 fusion.5
  414.8 9.8 %custom-call.6 = f32[1,128,128]{1,2,0:T(8,128)S(1)} custom-call(f32[1,128,128]{2,1,0:T(8,128)S(1)} %fusion.5), custom_call_target="InvertDiagBlocksLowerTriangular" | custom-call | tf_op jit(solution)/shard_map/triangular_solve | solution.py:18
  424.6 0.0 copy-done
  424.6 0.0 copy-start.1
  424.6 3.4 fusion.6
  428.0 0.0 copy-start.2
  428.0 1.3 copy-done.2
  429.4 0.0 copy-done.1
  429.4 2.2 convolution_bitcast_fusion.1
  431.6 0.0 all-reduce.9.cloned.1.call-update
  431.6 1.4 constant_dynamic-slice_fusion
  433.0 73.0 %all-reduce.9.cloned.1.call-done = f32[512,128]{0,1:T(8,128)} async-done(((f32[512,128]{0,1:T(8,128)}), f32[512,128]{0,1:T(8,128)}) %all-reduce.9.cloned.1.call-update) | async-done | bytes 262160 | tf_op jit(solution)/shard_map/psum | solution.py:38
  506.0 1.8 copy.6
  (1 shorter events, 0.0 us)
Async XLA Ops:
  7.2 310.6 %all-reduce.5.cloned.1.call-start = ((), (), s32[]{:S(2)}) async-start(), calls=%async_computation | async-start | bytes 4194304 | tf_op jit(solution)/shard_map/psum | solution.py:31
  47.1 352.8 %all-reduce.7.cloned.1.call-start = ((), (), s32[]{:S(2)}) async-start(), calls=%async_computation.1 | async-start | bytes 131072 | tf_op jit(solution)/shard_map/psum | solution.py:33
  317.8 106.8 %copy-start = (f32[4096,128]{0,1:T(8,128)S(1)}, f32[4096,128]{0,1:T(8,128)}, u32[]{:S(2)}) copy-start(f32[4096,128]{0,1:T(8,128)} %all-reduce.5.cloned.1.call-done) | copy-start | bytes 6291460
  322.6 183.4 %all-reduce.9.cloned.1.call-start = ((), (), s32[]{:S(2)}) async-start(), calls=%async_computation.2 | async-start | bytes 524288 | tf_op jit(solution)/shard_map/psum | solution.py:38
  424.6 4.8 copy-start.1
  428.0 1.4 copy-start.2
Sparse Core Ops, SparseCore 0:
  47.2 270.4 all-reduce.4
  322.7 77.1 all-reduce.6
  431.8 74.2 all-reduce.8
where the time goes:
time: 515 us; the launch traced here: 514 us
  waiting for transfers between devices  421 us (82%)
  blocking collectives  29.8 us (6%)
  other arithmetic  24.4 us (5%)
  matrix products  19.8 us (4%)
  between operations  13.8 us (3%)
  local copies, waits for them, and re-layouts  5.44 us (1%)
    psum x1, waiting for transfers between devices, per_device(): total_basis = lax.psum(local_basis, 'snap')  271 us
    psum x1, waiting for transfers between devices, per_device(): gram = lax.psum(local_gram, 'col')  77.1 us
    psum x1, waiting for transfers between devices, per_device(): scores = lax.psum(partial_scores, 'col')  73 us
    psum x1, blocking collectives, per_device(): sketch = lax.psum(partial_sketch, 'col').astype(jnp.bfloat16)  29.8 us
    another operation x3, other arithmetic, orthonormal(): lower = jnp.linalg.cholesky(gram)  12.4 us
    another operation x2, other arithmetic, orthonormal(): lax.linalg.triangular_solve(lower, range_basis, left_side=False, lower=Tr...  10.5 us
  transfers between devices with their start and end apart: 3, of which 3 were waited for; matrix products, arithmetic and copies ran while one was open for 0% of the time, Pallas kernels for 0%

commit v1 on v0

v1 whole, which is shorter than its diff:
```python
import functools

import jax
import jax.numpy as jnp
from jax import lax
from jax.experimental import pallas as pl
from jax.experimental.pallas import tpu as pltpu
from jax.sharding import PartitionSpec as P

RANK = 128
NX, NY, NZ, NC = 4, 4, 16, 2
NCOL = NY * NC
PLANE = NX * NCOL
ROWS = 64
TILE = NX * ROWS
LAG = 6
PANEL = 32
F32 = jnp.float32
HIGHEST = lax.Precision.HIGHEST
MESH = pl.DeviceIdType.MESH


def encode(value):
    top = jnp.maximum(jnp.max(jnp.abs(value), axis=0, keepdims=True), 1e-30)
    code = jnp.round(value * (32767.0 / top)).astype(jnp.int32).astype(jnp.int16)
    return code, top


def decode(code, top):
    return code.astype(jnp.int32).astype(F32) * (top * (1.0 / 32767.0))


def z_offset(j):
    return NZ // 2 + (1 - 2 * (j % 2)) * ((j + 1) // 2)


def factor_panel(m_ref, p):
    at = pl.multiple_of(p * PANEL, PANEL)
    g, e = m_ref[pl.ds(at, PANEL), :RANK], m_ref[pl.ds(at, PANEL), RANK:]
    g = pltpu.roll(g, lax.rem(RANK - at, RANK), 1)
    sub = lax.broadcasted_iota(jnp.int32, (PANEL, RANK), 0)
    lane = lax.broadcasted_iota(jnp.int32, (PANEL, RANK), 1)
    for j in range(0, PANEL, 2):
        c0 = jnp.broadcast_to(g[:, j : j + 1], (PANEL, RANK))
        c1 = jnp.broadcast_to(g[:, j + 1 : j + 2], (PANEL, RANK))
        a, b, d = c0[j : j + 1, :], c0[j + 1 : j + 2, :], c1[j + 1 : j + 2, :]
        b_over_a = b / a
        rest = d - b * b_over_a
        f1 = (c1 - c0 * b_over_a) / rest
        f0 = c0 / a - f1 * b_over_a
        below = sub > j + 1
        f0 = jnp.where(below, f0, jnp.where(sub == j + 1, b_over_a, 0.0))
        f1 = jnp.where(below, f1, 0.0)
        g, e = (
            g - f0 * g[j : j + 1, :] - f1 * g[j + 1 : j + 2, :],
            e - f0 * e[j : j + 1, :] - f1 * e[j + 1 : j + 2, :],
        )
    pivots = jnp.sum(jnp.where(sub == lane, g, 0.0), axis=1, keepdims=True)
    scale = lax.rsqrt(pivots)
    w, e = pltpu.roll(g * scale, at, 1), e * scale
    both = jnp.concatenate([w, e], axis=1)
    m_ref[pl.ds(at, PANEL), :] = both
    below = jnp.where(lane >= at + PANEL, w, 0.0)
    m_ref[...] -= lax.dot_general(below, both, (((0,), (0,)), ((), ())), precision=HIGHEST, preferred_element_type=F32)


def kernel(
    code_ref, a_hbm, scores_ref, eofs_ref,
    a, omega, half, core_in, y_in, sketch, sketch_t, tile,
    x_out, x_out_top, x_in, x_in_top, x_own,
    z_out, z_out_top, z_in, z_in_top, basis,
    all_code, all_top,
    gram_out, gram_in, gram_z, gram_all, system,
    proj, proj_sum, proj_in, proj_all,
    a_sem, core_sem, y_sem, s_sem,
    x_sem, x_top_sem, z_sem, z_top_sem,
    gz_sem, gz_top_sem, gx_sem, gx_top_sem,
    g1_sem, g2_sem, g3_sem, p1_sem, p2_sem,
):
    snap, col = lax.axis_index("snap"), lax.axis_index("col")
    z, x = snap // NX, snap % NX
    y, core = col // NC, col % NC
    place = x * NCOL + col

    def at_z(off):
        return {"snap": lax.rem(z + off, NZ) * NX + x, "col": col}

    def at_x(d):
        return {"snap": z * NX + lax.rem(x + d, NX), "col": col}

    def at_y(d):
        return {"snap": snap, "col": lax.rem(y + d, NY) * NC + core}

    def at_col(d):
        return {"snap": snap, "col": lax.rem(col + d, NCOL)}

    def at_plane(e):
        other = lax.rem(place + e, PLANE)
        return {"snap": z * NX + other // NCOL, "col": other % NCOL}

    other_core = {"snap": snap, "col": y * NC + (1 - core)}

    def remote(src, dst, sem, device):
        return pltpu.make_async_remote_copy(
            src_ref=src, dst_ref=dst, send_sem=sem[0], recv_sem=sem[1], device_id=device, device_id_type=MESH
        )

    def sems(ref, *index):
        return ref.at[(0, *index)], ref.at[(1, *index)]

    barrier = pltpu.get_barrier_semaphore()

    @pl.loop(1, PLANE)
    def _(e):
        pl.semaphore_signal(barrier, inc=1, device_id=at_plane(e), device_id_type=MESH)

    @pl.loop(1, NZ)
    def _(d):
        pl.semaphore_signal(barrier, inc=1, device_id=at_z(d), device_id_type=MESH)

    snaps = a.shape[0]
    kept = snaps // NC
    ranges = [pl.ds(pl.multiple_of((1 - core) * kept, kept), kept), pl.ds(pl.multiple_of(core * kept, kept), kept)]
    loads = [pltpu.make_async_copy(a_hbm.at[r], a.at[r], a_sem.at[i]) for i, r in enumerate(ranges)]
    for load in loads:
        load.start()

    width = 512

    @pl.loop(0, omega.shape[1] // width)
    def _(i):
        at = pl.ds(pl.multiple_of(i * width, width), width)
        code = code_ref[:, at]
        hits = lax.broadcasted_iota(jnp.int32, (RANK, width), 0) == code % RANK
        omega[:, at] = jnp.where(hits, jnp.where(code >= RANK, -1.0, 1.0), 0.0).astype(jnp.bfloat16)

    def sketch_rows(r):
        return lax.dot_general(a[r], omega[...], (((1,), (1,)), ((), ())), preferred_element_type=F32)

    loads[0].wait()
    half[0] = sketch_rows(ranges[0])
    pl.semaphore_wait(barrier, PLANE - 1 + NZ - 1)
    to_core = remote(half.at[0], core_in, sems(core_sem), other_core)
    to_core.start()
    loads[1].wait()
    mine = sketch_rows(ranges[1])
    to_core.wait()
    half[1] = mine + core_in[...]

    to_y = []
    for d in range(1, NY):
        rows = pl.ds(pl.multiple_of(lax.rem(y + d, NY) * ROWS, ROWS), ROWS)
        to_y.append(remote(half.at[1, rows], y_in.at[d - 1], sems(y_sem, d - 1), at_y(d)))
        to_y[-1].start()
    total = half[1, pl.ds(pl.multiple_of(y * ROWS, ROWS), ROWS), :]
    for d in range(1, NY):
        to_y[d - 1].wait_recv()
        total += y_in[d - 1]
    my_rows = pl.ds(pl.multiple_of(core * kept + y * ROWS, ROWS), ROWS)
    sketch[my_rows, :] = total.astype(jnp.bfloat16)
    for d in range(1, NCOL):
        remote(sketch.at[my_rows], sketch.at[my_rows], sems(s_sem, d - 1), at_col(d)).start()
    for copy in to_y:
        copy.wait_send()
    for d in range(1, NCOL):
        owner = lax.rem(col - d + NCOL, NCOL)
        rows = pl.ds(pl.multiple_of((owner % NC) * kept + (owner // NC) * ROWS, ROWS), ROWS)
        remote(sketch.at[rows], sketch.at[rows], sems(s_sem, d - 1), at_col(d)).wait()
    sketch_t[...] = sketch[...].astype(F32).T.astype(jnp.bfloat16)

    def x_copies(j, d):
        return (
            remote(x_out.at[j, d - 1], x_in.at[j, d - 1], sems(x_sem, j, d - 1), at_x(d)),
            remote(x_out_top.at[j, d - 1], x_in_top.at[j, d - 1], sems(x_top_sem, j, d - 1), at_x(d)),
        )

    def z_copies(j):
        return (
            remote(z_out.at[j], z_in.at[j], sems(z_sem, j), at_z(z_offset(j))),
            remote(z_out_top.at[j], z_in_top.at[j], sems(z_top_sem, j), at_z(z_offset(j))),
        )

    def tile_at(owner):
        return pl.ds(pl.multiple_of(owner * TILE, TILE), TILE)

    def produce(j):
        owner = lax.rem(z + z_offset(j), NZ)
        tile[...] = jnp.dot(sketch_t[...], a[:, tile_at(owner)], preferred_element_type=F32).T
        for d in range(1, NX):
            rows = pl.ds(pl.multiple_of(lax.rem(x + d, NX) * ROWS, ROWS), ROWS)
            x_out[j, d - 1], x_out_top[j, d - 1] = encode(tile[rows, :])
            for copy in x_copies(j, d):
                copy.start()
        x_own[j] = tile[pl.ds(pl.multiple_of(x * ROWS, ROWS), ROWS), :]

    def x_sum(j):
        total = x_own[j]
        for d in range(1, NX):
            for copy in x_copies(j, d):
                copy.wait()
            total += decode(x_in[j, d - 1], x_in_top[j, d - 1])
        return total

    def consume(j):
        z_out[j], z_out_top[j] = encode(x_sum(j))
        for copy in z_copies(j):
            copy.start()

    pl.loop(0, LAG)(produce)

    @pl.loop(LAG, NZ)
    def _(j):
        produce(j)
        consume(j - LAG)

    pl.loop(NZ - LAG, NZ - 1)(consume)
    basis[...] = x_sum(NZ - 1)

    @pl.loop(0, NZ - 1)
    def _(j):
        for copy in z_copies(j):
            copy.wait()
        basis[...] += decode(z_in[j], z_in_top[j])

    own = basis[...]
    gram = lax.dot_general(own, own, (((0,), (0,)), ((), ())), precision=HIGHEST, preferred_element_type=F32)
    for i in range(PLANE):
        gram_out[i] = gram[i * (RANK // PLANE) : (i + 1) * (RANK // PLANE), :]

    def g1_copy(e):
        return remote(gram_out.at[lax.rem(place + e, PLANE)], gram_in.at[e], sems(g1_sem, e), at_plane(e))

    @pl.loop(1, PLANE)
    def _(e):
        g1_copy(e).start()

    all_code[z, x], all_top[z, x] = encode(own)

    def gz_copies(owner, j):
        return (
            remote(all_code.at[owner, x], all_code.at[owner, x], sems(gz_sem, j), at_z(z_offset(j))),
            remote(all_top.at[owner, x], all_top.at[owner, x], sems(gz_top_sem, j), at_z(z_offset(j))),
        )

    def gx_copies(owner, j, d, source):
        return (
            remote(all_code.at[owner, source], all_code.at[owner, source], sems(gx_sem, j, d - 1), at_x(d)),
            remote(all_top.at[owner, source], all_top.at[owner, source], sems(gx_top_sem, j, d - 1), at_x(d)),
        )

    @pl.loop(0, NZ - 1)
    def _(j):
        for copy in gz_copies(z, j):
            copy.start()

    def forward(j):
        for d in range(1, NX):
            for copy in gx_copies(lax.rem(z - z_offset(j) + NZ, NZ), j, d, x):
                copy.start()

    def receive_and_forward(i):
        j = NZ - 2 - i
        for copy in gz_copies(lax.rem(z - z_offset(j) + NZ, NZ), j):
            copy.wait_recv()
        forward(j)

    forward(NZ - 1)

    gram_z[z] = gram_out[place]

    @pl.loop(1, PLANE)
    def _(e):
        g1_copy(e).wait_recv()
        gram_z[z] += gram_in[e]

    def g2_copy(owner, d):
        return remote(gram_z.at[owner], gram_z.at[owner], sems(g2_sem, d), at_z(d))

    @pl.loop(1, NZ)
    def _(d):
        g2_copy(z, d).start()

    pl.loop(0, NZ // 2)(receive_and_forward)

    @pl.loop(1, NZ)
    def _(d):
        g2_copy(lax.rem(z - d + NZ, NZ), d).wait_recv()

    gram_all[place] = jnp.sum(gram_z[...], axis=0)

    def g3_copy(owner, e):
        return remote(gram_all.at[owner], gram_all.at[owner], sems(g3_sem, e), at_plane(e))

    @pl.loop(1, PLANE)
    def _(e):
        g3_copy(place, e).start()

    pl.loop(NZ // 2, NZ - 1)(receive_and_forward)

    proj[...] = jnp.zeros_like(proj)

    @pl.loop(0, NZ)
    def _(i):
        j = NZ - 1 - i
        owner = lax.rem(z - z_offset(j) + NZ, NZ)
        for d in range(1, NX):
            for copy in gx_copies(owner, j, d, lax.rem(x - d + NX, NX)):
                copy.wait_recv()
        parts = [decode(all_code[owner, s], all_top[owner, s]) for s in range(NX)]
        value = jnp.concatenate(parts, axis=0)
        high = value.astype(jnp.bfloat16)
        low = (value - high.astype(F32)).astype(jnp.bfloat16)
        proj[...] += jnp.dot(
            a[:, tile_at(owner)], jnp.concatenate([high, low], axis=1), preferred_element_type=F32
        )

    def p1_copy(d):
        other = lax.rem(col + d, NCOL)
        rows = pl.ds(pl.multiple_of(other * ROWS, ROWS), ROWS)
        return remote(proj_sum.at[rows], proj_in.at[d - 1], sems(p1_sem, d - 1), at_col(d))

    proj_sum[...] = proj[:, :RANK] + proj[:, RANK:]
    for d in range(1, NCOL):
        p1_copy(d).start()

    @pl.loop(1, PLANE)
    def _(e):
        g3_copy(lax.rem(place - e + PLANE, PLANE), e).wait_recv()

    step = RANK // PLANE
    for i in range(PLANE):
        system[i * step : (i + 1) * step, :RANK] = gram_all[i]
    square = (RANK, RANK)
    system[:, RANK:] = jnp.where(
        lax.broadcasted_iota(jnp.int32, square, 0) == lax.broadcasted_iota(jnp.int32, square, 1), 1.0, 0.0
    )
    panels = RANK // PANEL
    pl.loop(0, panels // 2)(functools.partial(factor_panel, system))

    my_block = pl.ds(pl.multiple_of(col * ROWS, ROWS), ROWS)
    total = proj_sum[my_block, :]
    for d in range(1, NCOL):
        p1_copy(d).wait()
        total += proj_in[d - 1]
    proj_all[my_block, :] = total

    def p2_copy(d, owner):
        rows = pl.ds(pl.multiple_of(owner * ROWS, ROWS), ROWS)
        return remote(proj_all.at[rows], proj_all.at[rows], sems(p2_sem, d - 1), at_col(d))

    for d in range(1, NCOL):
        p2_copy(d, col).start()

    pl.loop(panels // 2, panels)(functools.partial(factor_panel, system))

    def whiten(value):
        return lax.dot_general(
            value, system[:, RANK:], (((1,), (1,)), ((), ())), precision=HIGHEST, preferred_element_type=F32
        )

    eofs_ref[...] = whiten(basis[...])
    for d in range(1, NCOL):
        p2_copy(d, lax.rem(col - d + NCOL, NCOL)).wait()
    scores_ref[...] = whiten(proj_all[...])

    @pl.loop(1, PLANE)
    def _(e):
        g1_copy(e).wait_send()
        g3_copy(place, e).wait_send()

    @pl.loop(1, NZ)
    def _(d):
        g2_copy(z, d).wait_send()

    @pl.loop(0, NZ - 1)
    def _(j):
        for copy in gz_copies(z, j):
            copy.wait_send()

    @pl.loop(0, NZ)
    def _(j):
        for d in range(1, NX):
            for copy in gx_copies(lax.rem(z - z_offset(j) + NZ, NZ), j, d, x):
                copy.wait_send()


def per_device(anomalies, sketch_code):
    snaps, cols = anomalies.shape
    vmem, dma = pltpu.VMEM, lambda *shape: pltpu.SemaphoreType.DMA((2, *shape))
    i16, bf16 = jnp.int16, jnp.bfloat16
    piece, top = (ROWS, RANK), (1, RANK)
    share = (RANK // PLANE, RANK)
    scratch = [
        vmem((snaps, cols), bf16),
        vmem((RANK, cols), bf16),
        vmem((2, snaps // NC, RANK), F32),
        vmem((snaps // NC, RANK), F32),
        vmem((NY - 1, *piece), F32),
        vmem((snaps, RANK), bf16),
        vmem((RANK, snaps), bf16),
        vmem((TILE, RANK), F32),
        vmem((NZ, NX - 1, *piece), i16),
        vmem((NZ, NX - 1, *top), F32),
        vmem((NZ, NX - 1, *piece), i16),
        vmem((NZ, NX - 1, *top), F32),
        vmem((NZ, *piece), F32),
        vmem((NZ - 1, *piece), i16),
        vmem((NZ - 1, *top), F32),
        vmem((NZ - 1, *piece), i16),
        vmem((NZ - 1, *top), F32),
        vmem(piece, F32),
        vmem((NZ, NX, *piece), i16),
        vmem((NZ, NX, *top), F32),
        vmem((PLANE, *share), F32),
        vmem((PLANE, *share), F32),
        vmem((NZ, *share), F32),
        vmem((PLANE, *share), F32),
        vmem((RANK, 2 * RANK), F32),
        vmem((snaps, 2 * RANK), F32),
        vmem((snaps, RANK), F32),
        vmem((NCOL - 1, *piece), F32),
        vmem((snaps, RANK), F32),
        pltpu.SemaphoreType.DMA((2,)),
        dma(),
        dma(NY - 1),
        dma(NCOL - 1),
        dma(NZ, NX - 1), dma(NZ, NX - 1),
        dma(NZ - 1), dma(NZ - 1),
        dma(NZ - 1), dma(NZ - 1),
        dma(NZ, NX - 1), dma(NZ, NX - 1),
        dma(PLANE), dma(NZ), dma(PLANE),
        dma(NCOL - 1), dma(NCOL - 1),
    ]
    return pl.pallas_call(
        kernel,
        out_shape=(jax.ShapeDtypeStruct((snaps, RANK), F32), jax.ShapeDtypeStruct(piece, F32)),
        in_specs=[pl.BlockSpec(memory_space=pltpu.VMEM), pl.BlockSpec(memory_space=pl.ANY)],
        out_specs=(pl.BlockSpec(memory_space=pltpu.VMEM), pl.BlockSpec(memory_space=pltpu.VMEM)),
        scratch_shapes=scratch,
        compiler_params=pltpu.CompilerParams(collective_id=0, has_side_effects=True, vmem_limit_bytes=48 << 20),
    )(sketch_code.reshape(1, cols), anomalies)


def solution(mesh):
    return jax.shard_map(
        per_device,
        mesh=mesh,
        in_specs=(P("snap", "col"), P("col")),
        out_specs=(P("snap", None), P(("col", "snap"), None)),
        check_vma=False,
    )
```

time: 515 us -> 99.1 us (0.19)
  waiting for transfers between devices: 421 us -> 0 us
  Pallas kernels: 0 us -> 94 us
  blocking collectives: 29.8 us -> 0 us
  other arithmetic: 24.4 us -> 0 us
  matrix products: 19.8 us -> 0 us
  between operations: 13.8 us -> 0.65 us
    psum x3 -> x0, waiting for transfers between devices: 421 us -> none  [the longest x1 271 us: per_device(): total_basis = lax.psum(local_basis, 'snap')]
    pallas_call x0 -> x1, Pallas kernels: none -> 94 us  [per_device(): pl.pallas_call(kernel, out_shape=(jax.ShapeDtypeStruct((snaps, RANK), F32...]
    psum x1 -> x0, blocking collectives: 29.8 us -> none  [per_device(): sketch = lax.psum(partial_sketch, 'col').astype(jnp.bfloat16)]
    another operation x5 -> x0, other arithmetic: 22.9 us -> none  [the longest x3 12.4 us: orthonormal(): lower = jnp.linalg.cholesky(gram)]
    dot_general x4 -> x0, matrix products: 16.4 us -> none  [the longest x1 5.12 us: per_device(): jnp.dot(anomalies, omega, preferred_element_type=jnp.float32)]
  transfers between devices with their start and end apart: 3 -> 0, of which waited for: 3 -> 0; matrix products, arithmetic and copies ran while one was open for 0% -> 0% of each run, Pallas kernels for 0% -> 0%
where the time goes in v1:
time: 99.1 us; the launch traced here: 98.9 us
  Pallas kernels  94 us (95%)
  local copies, waits for them, and re-layouts  4.22 us (4%)
    pallas_call x1, Pallas kernels, per_device(): pl.pallas_call(kernel, out_shape=(jax.ShapeDtypeStruct((snaps, RANK), F32...  94 us
    unnamed x6, local copies, waits for them, and re-layouts  4.22 us

profile of v1, /device:TPU:1, one launch (start us, length us, event | category | flops | bytes accessed | tf_op | source)
XLA Modules:
  0.0 98.9 jit_solution(8489587186180643619)
XLA Ops:
  0.6 0.0 copy-start
  0.6 2.2 %copy-done = bf16[512,4096]{1,0:T(8,128)(2,1)S(1)} copy-done((bf16[512,4096]{1,0:T(8,128)(2,1)S(1)}, bf16[512,4096]{1,0:T(8,128)(2,1)}, u32[]{:S(2)}) %copy-start) | copy-done | bytes 4194328
  2.8 0.0 copy-start.1
  2.8 0.7 copy-done.1
  3.5 94.0 %shard_map.41 = (f32[512,128]{1,0:T(8,128)S(1)}, f32[64,128]{1,0:T(8,128)S(1)}) custom-call(s32[1,4096]{1,0:T(1,128)S(1)} %bitcast.1, bf16[512,4096]{1,0:T(8,128)(2,1)S(1)} %copy-done), custom_call_target="tpu_custom_call" | custom-call | tf_op jit(solution)/shard_map/pallas_call | solution.py:434
  97.6 0.7 copy.6
  98.3 0.6 copy.7
Async XLA Ops:
  0.6 2.2 %copy-start = (bf16[512,4096]{1,0:T(8,128)(2,1)S(1)}, bf16[512,4096]{1,0:T(8,128)(2,1)}, u32[]{:S(2)}) copy-start(bf16[512,4096]{1,0:T(8,128)(2,1)} %a_hbm.1) | copy-start | bytes 12582916
  2.8 0.7 copy-start.1

commit v2 on v0

v2 whole, which is shorter than its diff:
```python
import functools

import jax
import jax.numpy as jnp
from jax import lax
from jax.experimental import pallas as pl
from jax.experimental.pallas import tpu as pltpu
from jax.sharding import PartitionSpec as P

RANK = 128
NX, NY, NZ, NC = 4, 4, 16, 2
NCOL = NY * NC
PLANE = NX * NCOL
ROWS = 64
TILE = NX * ROWS
LAG = 6
GROUP = 4
PANEL = 32
AHEAD = 8
F32 = jnp.float32
HIGHEST = lax.Precision.HIGHEST
MESH = pl.DeviceIdType.MESH
DIRECT, RELAYS, NEAR = (6, 10, 3, 13, 8, 1, 15), (3, 13, 6, 10), (1, 15)

(S_CORE, S_Y, S_Y_TOP, S_BACK, R_X, R_X_TOP, R_Z, R_Z_TOP, G_Z, G_Z_TOP, G_X, G_X_TOP,
 GRAM_PLANE, GRAM_Z, GRAM_BACK, P_CORE, P_Y, P_Y_TOP, P_BACK) = range(19)
GROUPS = 19


def encode(value):
    top = jnp.maximum(jnp.max(jnp.abs(value), axis=0, keepdims=True), 1e-30)
    code = jnp.round(value * (32767.0 / top)).astype(jnp.int32).astype(jnp.int16)
    return code, top


def decode(code, top):
    return code.astype(jnp.int32).astype(F32) * (top * (1.0 / 32767.0))


def z_offset(j):
    return NZ // 2 + (1 - 2 * (j % 2)) * ((j + 1) // 2)


def factor_panel(m_ref, p):
    at = pl.multiple_of(p * PANEL, PANEL)
    g, e = m_ref[pl.ds(at, PANEL), :RANK], m_ref[pl.ds(at, PANEL), RANK:]
    g = pltpu.roll(g, lax.rem(RANK - at, RANK), 1)
    sub = lax.broadcasted_iota(jnp.int32, (PANEL, RANK), 0)
    lane = lax.broadcasted_iota(jnp.int32, (PANEL, RANK), 1)
    scale = jnp.zeros((PANEL, RANK), F32)
    for j in range(0, PANEL, AHEAD):
        columns = [jnp.broadcast_to(g[:, j + k : j + k + 1], (PANEL, RANK)) for k in range(AHEAD)]
        for k in range(AHEAD):
            row = j + k
            pivot = columns[k][row : row + 1, :]
            scale = jnp.where(sub == row, lax.rsqrt(pivot), scale)
            factor = jnp.where(sub > row, columns[k] * (1.0 / pivot), 0.0)
            for later in range(k + 1, AHEAD):
                columns[later] -= factor * columns[later][row : row + 1, :]
            g -= factor * g[row : row + 1, :]
            e -= factor * e[row : row + 1, :]
    w, e = pltpu.roll(g * scale, at, 1), e * scale
    both = jnp.concatenate([w, e], axis=1)
    m_ref[pl.ds(at, PANEL), :] = both
    below = jnp.where(lane >= at + PANEL, w, 0.0)
    m_ref[...] -= lax.dot_general(below, both, (((0,), (0,)), ((), ())), precision=HIGHEST, preferred_element_type=F32)


def kernel(
    code_hbm, a_hbm, scores_ref, eofs_ref,
    code_ref, a, omega, half, core_in, y_code, y_top, sketch, sketch_t, tile,
    x_out, x_out_top, x_in, x_in_top, x_own,
    z_out, z_out_top, z_in, z_in_top, basis,
    all_code, all_top,
    gram_out, gram_in, gram_z, gram_all, system,
    split, proj, proj_half, proj_in, proj_code, proj_top, proj_all,
    load_sem, send, recv, x_sem, x_top_sem, gz_sem, gx_sem,
):
    snap, col = lax.axis_index("snap"), lax.axis_index("col")
    z, x = snap // NX, snap % NX
    y, core = col // NC, col % NC
    place = x * NCOL + col

    def at_z(off):
        return {"snap": lax.rem(z + off, NZ) * NX + x, "col": col}

    def at_x(d):
        return {"snap": z * NX + lax.rem(x + d, NX), "col": col}

    def at_y(d):
        return {"snap": snap, "col": lax.rem(y + d, NY) * NC + core}

    def at_plane(e):
        other = lax.rem(place + e, PLANE)
        return {"snap": z * NX + other // NCOL, "col": other % NCOL}

    other_core = {"snap": snap, "col": y * NC + (1 - core)}

    def remote(src, dst, group, device, recv_sem=None):
        return pltpu.make_async_remote_copy(
            src_ref=src,
            dst_ref=dst,
            send_sem=send.at[group],
            recv_sem=recv.at[group] if recv_sem is None else recv_sem,
            device_id=device,
            device_id_type=MESH,
        )

    def wait_recv(region, group, recv_sem=None):
        remote(region, region, group, other_core, recv_sem).wait_recv()

    def wait_send(region, group):
        remote(region, region, group, other_core).wait_send()

    barrier = pltpu.get_barrier_semaphore()

    snaps = a.shape[0]
    kept = snaps // NC
    other_rows = pl.ds(pl.multiple_of((1 - core) * kept, kept), kept)
    core_rows = pl.ds(pl.multiple_of(core * kept, kept), kept)
    loads = [pltpu.make_async_copy(code_hbm, code_ref, load_sem.at[0])]
    loads += [pltpu.make_async_copy(a_hbm.at[r], a.at[r], load_sem.at[1 + i]) for i, r in enumerate((other_rows, core_rows))]
    for load in loads:
        load.start()

    @pl.loop(1, PLANE)
    def _(e):
        pl.semaphore_signal(barrier, inc=1, device_id=at_plane(e), device_id_type=MESH)

    @pl.loop(1, NZ)
    def _(d):
        pl.semaphore_signal(barrier, inc=1, device_id=at_z(d), device_id_type=MESH)

    width = 512
    loads[0].wait()

    @pl.loop(0, omega.shape[1] // width)
    def _(i):
        at = pl.ds(pl.multiple_of(i * width, width), width)
        code = code_ref[:, at]
        hits = lax.broadcasted_iota(jnp.int32, (RANK, width), 0) == code % RANK
        omega[:, at] = jnp.where(hits, jnp.where(code >= RANK, -1.0, 1.0), 0.0).astype(jnp.bfloat16)

    def sketch_rows(r):
        return lax.dot_general(a[r], omega[...], (((1,), (1,)), ((), ())), preferred_element_type=F32)

    loads[1].wait()
    half[...] = sketch_rows(other_rows)
    pl.semaphore_wait(barrier, PLANE - 1 + NZ - 1)
    to_core = remote(half, core_in, S_CORE, other_core)
    to_core.start()
    loads[2].wait()
    mine = sketch_rows(core_rows)

    def sum_over_y(value, code_buffer, top_buffer, group):
        code_buffer[y], top_buffer[y] = encode(value)
        for d in range(1, NY):
            remote(code_buffer.at[y], code_buffer.at[y], group, at_y(d)).start()
            remote(top_buffer.at[y], top_buffer.at[y], group + 1, at_y(d)).start()

    def summed_over_y(code_buffer, top_buffer, group):
        for k, buffer in enumerate((code_buffer, top_buffer)):
            wait_recv(buffer.at[pl.ds(0, NY - 1)], group + k)
            wait_send(buffer.at[pl.ds(0, NY - 1)], group + k)
        return sum(decode(code_buffer[i], top_buffer[i]) for i in range(NY))

    to_core.wait_recv()
    sum_over_y(mine + core_in[...], y_code, y_top, S_Y)
    to_core.wait_send()
    sketch[core_rows, :] = summed_over_y(y_code, y_top, S_Y).astype(jnp.bfloat16)
    remote(sketch.at[core_rows], sketch.at[core_rows], S_BACK, other_core).start()
    wait_recv(sketch.at[other_rows], S_BACK)
    sketch_t[...] = sketch[...].astype(F32).T.astype(jnp.bfloat16)
    wait_send(sketch.at[core_rows], S_BACK)

    def z_copies(j):
        return (
            remote(z_out.at[j], z_in.at[j], R_Z, at_z(z_offset(j))),
            remote(z_out_top.at[j], z_in_top.at[j], R_Z_TOP, at_z(z_offset(j))),
        )

    def tile_at(owner):
        return pl.ds(pl.multiple_of(owner * TILE, TILE), TILE)

    def produce(j):
        owner = lax.rem(z + z_offset(j), NZ)
        tile[...] = jnp.dot(sketch_t[...], a[:, tile_at(owner)], preferred_element_type=F32).T
        for d in range(1, NX):
            rows = pl.ds(pl.multiple_of(lax.rem(x + d, NX) * ROWS, ROWS), ROWS)
            x_out[j, d - 1], x_out_top[j, d - 1] = encode(tile[rows, :])
            remote(x_out.at[j, d - 1], x_in.at[j, d - 1], R_X, at_x(d), x_sem.at[j]).start()
            remote(x_out_top.at[j, d - 1], x_in_top.at[j, d - 1], R_X_TOP, at_x(d), x_top_sem.at[j]).start()
        x_own[j] = tile[pl.ds(pl.multiple_of(x * ROWS, ROWS), ROWS), :]

    def x_sum(j):
        wait_recv(x_in.at[j], R_X, x_sem.at[j])
        wait_recv(x_in_top.at[j], R_X_TOP, x_top_sem.at[j])
        total = x_own[j]
        for d in range(1, NX):
            total += decode(x_in[j, d - 1], x_in_top[j, d - 1])
        return total

    def consume(j):
        z_out[j], z_out_top[j] = encode(x_sum(j))
        for copy in z_copies(j):
            copy.start()

    pl.loop(0, LAG)(produce)

    @pl.loop(LAG, NZ)
    def _(j):
        produce(j)
        consume(j - LAG)

    pl.loop(NZ - LAG, NZ - 1)(consume)
    basis[...] = x_sum(NZ - 1)
    wait_recv(z_in, R_Z)
    wait_recv(z_in_top, R_Z_TOP)

    @pl.loop(0, NZ - 1)
    def _(j):
        basis[...] += decode(z_in[j], z_in_top[j])

    own = basis[...]
    all_code[z, x], all_top[x, z] = encode(own)

    def gather_z(offset, d):
        chunk = all_code.at[lax.rem(z - offset + NZ, NZ), x]
        remote(chunk, chunk, G_Z, at_z(d), gz_sem.at[(offset + d) % NZ]).start()

    def gather_x(offset):
        chunk = all_code.at[lax.rem(z - offset + NZ, NZ), x]
        for d in range(1, NX):
            remote(chunk, chunk, G_X, at_x(d), gx_sem.at[offset]).start()

    def arrived(offset):
        wait_recv(all_code.at[lax.rem(z - offset + NZ, NZ), x], G_Z, gz_sem.at[offset])

    for d in DIRECT:
        gather_z(0, d)

    @pl.loop(1, NZ)
    def _(d):
        remote(all_top.at[x, z], all_top.at[x, z], G_Z_TOP, at_z(d)).start()

    gather_x(0)

    gram = lax.dot_general(own, own, (((0,), (0,)), ((), ())), precision=HIGHEST, preferred_element_type=F32)
    share = RANK // PLANE
    for i in range(PLANE):
        gram_out[i] = gram[i * share : (i + 1) * share, :]

    @pl.loop(1, PLANE)
    def _(e):
        remote(gram_out.at[lax.rem(place + e, PLANE)], gram_in.at[e - 1], GRAM_PLANE, at_plane(e)).start()

    for offset in (1, 15):
        arrived(offset)
        gather_x(offset)

    def relay(offset):
        arrived(offset)
        for d in NEAR:
            gather_z(offset, d)
        gather_x(offset)

    for offset in RELAYS[:2]:
        relay(offset)

    wait_recv(gram_in, GRAM_PLANE)
    gram_z[z] = gram_out[place] + jnp.sum(gram_in[...], axis=0)

    @pl.loop(1, NZ)
    def _(d):
        remote(gram_z.at[z], gram_z.at[z], GRAM_Z, at_z(d)).start()

    for offset in RELAYS[2:]:
        relay(offset)
    for offset in (2, 4, 14, 12, 8):
        arrived(offset)
        gather_x(offset)
    wait_recv(all_top.at[0, pl.ds(0, NZ - 1)], G_Z_TOP)
    for d in range(1, NX):
        remote(all_top.at[x], all_top.at[x], G_X_TOP, at_x(d)).start()
    for offset in (5, 7, 11, 9):
        arrived(offset)
        gather_x(offset)

    wait_recv(gram_z.at[pl.ds(0, NZ - 1)], GRAM_Z)
    gram_all[place] = jnp.sum(gram_z[...], axis=0)

    @pl.loop(1, PLANE)
    def _(e):
        remote(gram_all.at[place], gram_all.at[place], GRAM_BACK, at_plane(e)).start()

    proj[...] = jnp.zeros_like(proj)
    wait_recv(all_top.at[pl.ds(0, NX - 1)], G_X_TOP)

    @pl.loop(0, NZ // GROUP)
    def _(i):
        first = lax.rem(z // GROUP + i, NZ // GROUP) * GROUP

        @pl.loop(0, GROUP)
        def _(t):
            owner = first + t
            wait_recv(all_code.at[owner, pl.ds(0, NX - 1)], G_X, gx_sem.at[lax.rem(z - owner + NZ, NZ)])
            for s in range(NX):
                value = decode(all_code[owner, s], all_top[s, owner])
                high = value.astype(jnp.bfloat16)
                rows = pl.ds(pl.multiple_of((t * NX + s) * ROWS, ROWS), ROWS)
                split[rows, :RANK] = high
                split[rows, RANK:] = (value - high.astype(F32)).astype(jnp.bfloat16)

        columns = pl.ds(pl.multiple_of(first * TILE, GROUP * TILE), GROUP * TILE)
        proj[...] += jnp.dot(a[:, columns], split[...], preferred_element_type=F32)

    proj_half[...] = proj[other_rows, :RANK] + proj[other_rows, RANK:]
    remote(proj_half, proj_in, P_CORE, other_core).start()
    mine = proj[core_rows, :RANK] + proj[core_rows, RANK:]
    wait_recv(proj_in, P_CORE)
    sum_over_y(mine + proj_in[...], proj_code, proj_top, P_Y)

    wait_recv(gram_all.at[pl.ds(0, PLANE - 1)], GRAM_BACK)
    for i in range(PLANE):
        system[i * share : (i + 1) * share, :RANK] = gram_all[i]
    square = (RANK, RANK)
    system[:, RANK:] = jnp.where(
        lax.broadcasted_iota(jnp.int32, square, 0) == lax.broadcasted_iota(jnp.int32, square, 1), 1.0, 0.0
    )
    panels = RANK // PANEL
    pl.loop(0, panels // 2)(functools.partial(factor_panel, system))

    proj_all[core_rows, :] = summed_over_y(proj_code, proj_top, P_Y)
    remote(proj_all.at[core_rows], proj_all.at[core_rows], P_BACK, other_core).start()

    pl.loop(panels // 2, panels)(functools.partial(factor_panel, system))

    def whiten(value):
        return lax.dot_general(
            value, system[:, RANK:], (((1,), (1,)), ((), ())), precision=HIGHEST, preferred_element_type=F32
        )

    eofs_ref[...] = whiten(basis[...])
    wait_recv(proj_all.at[other_rows], P_BACK)
    scores_ref[...] = whiten(proj_all[...])

    wait_send(x_out, R_X)
    wait_send(x_out_top, R_X_TOP)
    wait_send(z_out, R_Z)
    wait_send(z_out_top, R_Z_TOP)
    wait_send(z_in, G_Z)
    wait_send(x_in, G_X)
    wait_send(z_in_top, G_Z_TOP)
    wait_send(all_top.at[pl.ds(0, NX - 1)], G_X_TOP)
    wait_send(gram_in, GRAM_PLANE)
    wait_send(gram_z.at[pl.ds(0, NZ - 1)], GRAM_Z)
    wait_send(gram_in, GRAM_BACK)
    wait_send(proj_half, P_CORE)
    wait_send(proj_all.at[core_rows], P_BACK)


def per_device(anomalies, sketch_code):
    snaps, cols = anomalies.shape
    vmem, dma = pltpu.VMEM, lambda *shape: pltpu.SemaphoreType.DMA(shape)
    i16, bf16 = jnp.int16, jnp.bfloat16
    piece, top = (ROWS, RANK), (1, RANK)
    share = (RANK // PLANE, RANK)
    kept = (snaps // NC, RANK)
    scratch = [
        vmem((1, cols), jnp.int32),
        vmem((snaps, cols), bf16),
        vmem((RANK, cols), bf16),
        vmem(kept, F32),
        vmem(kept, F32),
        vmem((NY, *kept), i16),
        vmem((NY, *top), F32),
        vmem((snaps, RANK), bf16),
        vmem((RANK, snaps), bf16),
        vmem((TILE, RANK), F32),
        vmem((NZ, NX - 1, *piece), i16),
        vmem((NZ, NX - 1, *top), F32),
        vmem((NZ, NX - 1, *piece), i16),
        vmem((NZ, NX - 1, *top), F32),
        vmem((NZ, *piece), F32),
        vmem((NZ - 1, *piece), i16),
        vmem((NZ - 1, *top), F32),
        vmem((NZ - 1, *piece), i16),
        vmem((NZ - 1, *top), F32),
        vmem(piece, F32),
        vmem((NZ, NX, *piece), i16),
        vmem((NX, NZ, *top), F32),
        vmem((PLANE, *share), F32),
        vmem((PLANE - 1, *share), F32),
        vmem((NZ, *share), F32),
        vmem((PLANE, *share), F32),
        vmem((RANK, 2 * RANK), F32),
        vmem((GROUP * TILE, 2 * RANK), bf16),
        vmem((snaps, 2 * RANK), F32),
        vmem(kept, F32),
        vmem(kept, F32),
        vmem((NY, *kept), i16),
        vmem((NY, *top), F32),
        vmem((snaps, RANK), F32),
        dma(3), dma(GROUPS), dma(GROUPS),
        dma(NZ), dma(NZ), dma(NZ), dma(NZ),
    ]
    return pl.pallas_call(
        kernel,
        out_shape=(jax.ShapeDtypeStruct((snaps, RANK), F32), jax.ShapeDtypeStruct(piece, F32)),
        in_specs=[pl.BlockSpec(memory_space=pltpu.HBM)] * 2,
        out_specs=(pl.BlockSpec(memory_space=pltpu.VMEM), pl.BlockSpec(memory_space=pltpu.VMEM)),
        scratch_shapes=scratch,
        compiler_params=pltpu.CompilerParams(collective_id=0, has_side_effects=True, vmem_limit_bytes=48 << 20),
    )(sketch_code.reshape(1, cols), anomalies)


def solution(mesh):
    return jax.shard_map(
        per_device,
        mesh=mesh,
        in_specs=(P("snap", "col"), P("col")),
        out_specs=(P("snap", None), P(("col", "snap"), None)),
        check_vma=False,
    )
```

time: 515 us -> 84.3 us (0.16)
  waiting for transfers between devices: 421 us -> 0 us
  Pallas kernels: 0 us -> 79.2 us
  blocking collectives: 29.8 us -> 0 us
  other arithmetic: 24.4 us -> 0 us
  matrix products: 19.8 us -> 0 us
  between operations: 13.8 us -> 0.65 us
    psum x3 -> x0, waiting for transfers between devices: 421 us -> none  [the longest x1 271 us: per_device(): total_basis = lax.psum(local_basis, 'snap')]
    pallas_call x0 -> x1, Pallas kernels: none -> 79.2 us  [per_device(): pl.pallas_call(kernel, out_shape=(jax.ShapeDtypeStruct((snaps, RANK), F32...]
    psum x1 -> x0, blocking collectives: 29.8 us -> none  [per_device(): sketch = lax.psum(partial_sketch, 'col').astype(jnp.bfloat16)]
    another operation x5 -> x0, other arithmetic: 22.9 us -> none  [the longest x3 12.4 us: orthonormal(): lower = jnp.linalg.cholesky(gram)]
    dot_general x4 -> x0, matrix products: 16.4 us -> none  [the longest x1 5.12 us: per_device(): jnp.dot(anomalies, omega, preferred_element_type=jnp.float32)]
  transfers between devices with their start and end apart: 3 -> 0, of which waited for: 3 -> 0; matrix products, arithmetic and copies ran while one was open for 0% -> 0% of each run, Pallas kernels for 0% -> 0%
where the time goes in v2:
time: 84.3 us; the launch traced here: 84.1 us
  Pallas kernels  79.2 us (94%)
  local copies, waits for them, and re-layouts  4.22 us (5%)
    pallas_call x1, Pallas kernels, per_device(): pl.pallas_call(kernel, out_shape=(jax.ShapeDtypeStruct((snaps, RANK), F32...  79.2 us
    unnamed x6, local copies, waits for them, and re-layouts  4.22 us

profile of v2, /device:TPU:1, one launch (start us, length us, event | category | flops | bytes accessed | tf_op | source)
XLA Modules:
  0.0 84.1 jit_solution(5374873260436482243)
XLA Ops:
  0.6 0.0 copy-start
  0.6 2.2 %copy-done = bf16[512,4096]{1,0:T(8,128)(2,1)S(1)} copy-done((bf16[512,4096]{1,0:T(8,128)(2,1)S(1)}, bf16[512,4096]{1,0:T(8,128)(2,1)}, u32[]{:S(2)}) %copy-start) | copy-done | bytes 4194328
  2.8 0.0 copy-start.1
  2.8 0.7 copy-done.1
  3.5 79.2 %shard_map.41 = (f32[512,128]{1,0:T(8,128)S(1)}, f32[64,128]{1,0:T(8,128)S(1)}) custom-call(s32[1,4096]{1,0:T(1,128)S(1)} %bitcast.1, bf16[512,4096]{1,0:T(8,128)(2,1)S(1)} %copy-done), custom_call_target="tpu_custom_call" | custom-call | tf_op jit(solution)/shard_map/pallas_call | solution.py:407
  82.8 0.7 copy.6
  83.5 0.6 copy.7
Async XLA Ops:
  0.6 2.2 %copy-start = (bf16[512,4096]{1,0:T(8,128)(2,1)S(1)}, bf16[512,4096]{1,0:T(8,128)(2,1)}, u32[]{:S(2)}) copy-start(bf16[512,4096]{1,0:T(8,128)(2,1)} %a_hbm.1) | copy-start | bytes 12582916
  2.8 0.7 copy-start.1

commit v3 on v2

--- a/solution.py
+++ b/solution.py
@@ -20,7 +20,7 @@
 F32 = jnp.float32
 HIGHEST = lax.Precision.HIGHEST
 MESH = pl.DeviceIdType.MESH
-DIRECT, RELAYS, NEAR = (6, 10, 3, 13, 8, 1, 15), (3, 13, 6, 10), (1, 15)
+DIRECT, RELAYS, NEAR = (1, 15, 8, 4, 12, 2), (4, 12, 8), (1, 15, 2)
 
 (S_CORE, S_Y, S_Y_TOP, S_BACK, R_X, R_X_TOP, R_Z, R_Z_TOP, G_Z, G_Z_TOP, G_X, G_X_TOP,
  GRAM_PLANE, GRAM_Z, GRAM_BACK, P_CORE, P_Y, P_Y_TOP, P_BACK) = range(19)
@@ -236,14 +236,8 @@
     def arrived(offset):
         wait_recv(all_code.at[lax.rem(z - offset + NZ, NZ), x], G_Z, gz_sem.at[offset])
 
-    for d in DIRECT:
+    for d in DIRECT[:5]:
         gather_z(0, d)
-
-    @pl.loop(1, NZ)
-    def _(d):
-        remote(all_top.at[x, z], all_top.at[x, z], G_Z_TOP, at_z(d)).start()
-
-    gather_x(0)
 
     gram = lax.dot_general(own, own, (((0,), (0,)), ((), ())), precision=HIGHEST, preferred_element_type=F32)
     share = RANK // PLANE
@@ -253,6 +247,15 @@
     @pl.loop(1, PLANE)
     def _(e):
         remote(gram_out.at[lax.rem(place + e, PLANE)], gram_in.at[e - 1], GRAM_PLANE, at_plane(e)).start()
+
+    for d in DIRECT[5:]:
+        gather_z(0, d)
+
+    @pl.loop(1, NZ)
+    def _(d):
+        remote(all_top.at[x, z], all_top.at[x, z], G_Z_TOP, at_z(d)).start()
+
+    gather_x(0)
 
     for offset in (1, 15):
         arrived(offset)
@@ -276,13 +279,13 @@
 
     for offset in RELAYS[2:]:
         relay(offset)
-    for offset in (2, 4, 14, 12, 8):
+    for offset in (2, 3, 5, 13, 11):
         arrived(offset)
         gather_x(offset)
     wait_recv(all_top.at[0, pl.ds(0, NZ - 1)], G_Z_TOP)
     for d in range(1, NX):
         remote(all_top.at[x], all_top.at[x], G_X_TOP, at_x(d)).start()
-    for offset in (5, 7, 11, 9):
+    for offset in (6, 14, 7, 9, 10):
         arrived(offset)
         gather_x(offset)
 
@@ -327,22 +330,20 @@
     system[:, RANK:] = jnp.where(
         lax.broadcasted_iota(jnp.int32, square, 0) == lax.broadcasted_iota(jnp.int32, square, 1), 1.0, 0.0
     )
-    panels = RANK // PANEL
-    pl.loop(0, panels // 2)(functools.partial(factor_panel, system))
+    pl.loop(0, RANK // PANEL)(functools.partial(factor_panel, system))
 
     proj_all[core_rows, :] = summed_over_y(proj_code, proj_top, P_Y)
     remote(proj_all.at[core_rows], proj_all.at[core_rows], P_BACK, other_core).start()
-
-    pl.loop(panels // 2, panels)(functools.partial(factor_panel, system))
 
     def whiten(value):
         return lax.dot_general(
             value, system[:, RANK:], (((1,), (1,)), ((), ())), precision=HIGHEST, preferred_element_type=F32
         )
 
+    scores_ref[core_rows, :] = whiten(proj_all[core_rows, :])
     eofs_ref[...] = whiten(basis[...])
     wait_recv(proj_all.at[other_rows], P_BACK)
-    scores_ref[...] = whiten(proj_all[...])
+    scores_ref[other_rows, :] = whiten(proj_all[other_rows, :])
 
     wait_send(x_out, R_X)
     wait_send(x_out_top, R_X_TOP)
@@ -410,7 +411,7 @@
         in_specs=[pl.BlockSpec(memory_space=pltpu.HBM)] * 2,
         out_specs=(pl.BlockSpec(memory_space=pltpu.VMEM), pl.BlockSpec(memory_space=pltpu.VMEM)),
         scratch_shapes=scratch,
-        compiler_params=pltpu.CompilerParams(collective_id=0, has_side_effects=True, vmem_limit_bytes=48 << 20),
+        compiler_params=pltpu.CompilerParams(collective_id=0, has_side_effects=True, vmem_limit_bytes=52 << 20),
     )(sketch_code.reshape(1, cols), anomalies)
 
 

time: 84.3 us -> 77 us (0.913)
  Pallas kernels: 79.2 us -> 74.1 us
  local copies, waits for them, and re-layouts: 4.22 us -> 2.03 us
    pallas_call x1, Pallas kernels: 79.2 us -> 74.1 us  [per_device(): pl.pallas_call(kernel, out_shape=(jax.ShapeDtypeStruct((snaps, RANK), F32...]
    unnamed x6 -> x4, local copies, waits for them, and re-layouts: 4.22 us -> 2.03 us
where the time goes in v3:
time: 77 us; the launch traced here: 76.8 us
  Pallas kernels  74.1 us (96%)
  local copies, waits for them, and re-layouts  2.03 us (3%)
    pallas_call x1, Pallas kernels, per_device(): pl.pallas_call(kernel, out_shape=(jax.ShapeDtypeStruct((snaps, RANK), F32...  74.1 us
    unnamed x4, local copies, waits for them, and re-layouts  2.03 us

profile of v3, /device:TPU:1, one launch (start us, length us, event | category | flops | bytes accessed | tf_op | source)
XLA Modules:
  0.0 76.8 jit_solution(427841719437961196)
XLA Ops:
  0.6 0.0 copy-start
  0.6 0.7 copy-done
  1.3 74.1 %shard_map.41 = (f32[512,128]{1,0:T(8,128)S(1)}, f32[64,128]{1,0:T(8,128)S(1)}) custom-call(s32[1,4096]{1,0:T(1,128)S(1)} %bitcast.1, bf16[512,4096]{1,0:T(8,128)(2,1)} %a_hbm.1), custom_call_target="tpu_custom_call" | custom-call | tf_op jit(solution)/shard_map/pallas_call | solution.py:408
  75.5 0.7 copy.6
  76.2 0.6 copy.7
Async XLA Ops:
  0.6 0.7 copy-start

commit v4 on v3

--- a/solution.py
+++ b/solution.py
@@ -217,16 +217,19 @@
     wait_recv(z_in, R_Z)
     wait_recv(z_in_top, R_Z_TOP)
 
-    @pl.loop(0, NZ - 1)
-    def _(j):
-        basis[...] += decode(z_in[j], z_in_top[j])
+    total = basis[...]
+    for j in range(NZ - 1):
+        total += decode(z_in[j], z_in_top[j])
+    basis[...] = total
 
     own = basis[...]
     all_code[z, x], all_top[x, z] = encode(own)
 
     def gather_z(offset, d):
-        chunk = all_code.at[lax.rem(z - offset + NZ, NZ), x]
-        remote(chunk, chunk, G_Z, at_z(d), gz_sem.at[(offset + d) % NZ]).start()
+        owner = lax.rem(z - offset + NZ, NZ)
+        chunk = all_code.at[owner, x]
+        step = 2 + (NZ - 4) * lax.rem(owner, 2) if d == 2 else d
+        remote(chunk, chunk, G_Z, at_z(step), gz_sem.at[lax.rem(offset + step, NZ)]).start()
 
     def gather_x(offset):
         chunk = all_code.at[lax.rem(z - offset + NZ, NZ), x]

time: 77 us -> 76.8 us (level)
  no operation moved by 1% of the time
where the time goes in v4:
time: 76.8 us; the launch traced here: 76.7 us
  Pallas kernels  74 us (96%)
  local copies, waits for them, and re-layouts  2.03 us (3%)
    pallas_call x1, Pallas kernels, per_device(): pl.pallas_call(kernel, out_shape=(jax.ShapeDtypeStruct((snaps, RANK), F32...  74 us
    unnamed x4, local copies, waits for them, and re-layouts  2.03 us

profile of v4, /device:TPU:1, one launch (start us, length us, event | category | flops | bytes accessed | tf_op | source)
XLA Modules:
  0.0 76.7 jit_solution(5966294600781116019)
XLA Ops:
  0.6 0.0 copy-start
  0.6 0.7 copy-done
  1.3 74.0 %shard_map.41 = (f32[512,128]{1,0:T(8,128)S(1)}, f32[64,128]{1,0:T(8,128)S(1)}) custom-call(s32[1,4096]{1,0:T(1,128)S(1)} %bitcast.1, bf16[512,4096]{1,0:T(8,128)(2,1)} %a_hbm.1), custom_call_target="tpu_custom_call" | custom-call | tf_op jit(solution)/shard_map/pallas_call | solution.py:411
  75.3 0.7 copy.6
  76.1 0.6 copy.7
Async XLA Ops:
  0.6 0.7 copy-start
